TPU v7x, 256 devices: a whole 4x4x8 slice. The times are simulated.
256 devices in a mesh: row: 4 (over z_hi), col: 16 (over z_lo, y, core), layer: 4 (over x).
Axes of the slice: x: 4, y: 4, z: 8 (z_hi: 4, z_lo: 2; z = z_hi * 2 + z_lo), core: 2. Of those that a mesh axis runs over, the one named last changes fastest.
Arguments:
- x_tiles: bfloat16 [8, 256, 2, 128, 128], P('layer', ('row', 'col')), may hold values from -1 to 1
- x_cols: int32 [8, 256, 2], P('layer', ('row', 'col')), may hold values from 0 to 511, as said below
- c_list: int32 [4, 16, 256, 2], P('row', 'col'), may hold values from 0 to 63, as said below
- c_count: int32 [4, 16], P('row', 'col'), may hold values from 1 to 256, as said below
Outputs:
- c_tiles: float32 [4, 16, 256, 128, 128], P('row', 'col', 'layer')
Inputs may be any that keep to these rules, and one draw needn't show every extreme that they name: `x_cols`: inside one section the 2 column indices of a block row are distinct. `c_list`: the first entry indexes the 64 block rows of the grid row, the second the 16 block rows of the grid column; the slots of one grid position hold distinct pairs. `c_count`: some grid position has all 256 slots live in every draw.
All inputs are finite; a program needn't handle non-finite values.
Results may differ from a plain program's by a relative error of at most 0.011.
Values may be sent and summed in bfloat16 or wider, within the bound.
A program may use at most 128 MiB of HBM per device.

v0:
```python
import math

import jax
import jax.numpy as jnp
from jax import lax
from jax.sharding import PartitionSpec as P


def accumulate(a_tiles, a_cols, b_tiles, b_cols, slot_pairs, live_count):
    total_slots = slot_pairs.shape[0]
    edge = a_tiles.shape[-1]
    per_round = math.gcd(32, total_slots)

    def one_round(round_index, partial_value):
        first_slot = round_index * per_round
        chosen_rows = lax.dynamic_slice_in_dim(slot_pairs, first_slot, per_round, 0)
        left_tiles = jnp.take(a_tiles, chosen_rows[:, 0], axis=1)
        right_tiles = jnp.take(b_tiles, chosen_rows[:, 1], axis=1)
        left_cols = jnp.take(a_cols, chosen_rows[:, 0], axis=1)
        right_cols = jnp.take(b_cols, chosen_rows[:, 1], axis=1)
        matches = left_cols[:, :, :, None] == right_cols[:, :, None, :]
        picked = jnp.sum(
            jnp.where(
                matches[..., None, None], right_tiles[:, :, None], jnp.zeros((), jnp.bfloat16)
            ),
            axis=3,
        )
        product = jnp.einsum(
            "sgpik,sgpjk->gij", left_tiles, picked, preferred_element_type=jnp.float32
        )
        live_mask = first_slot + jnp.arange(per_round, dtype=jnp.int32) < live_count
        product = jnp.where(live_mask[:, None, None], product, jnp.float32(0.0))
        return lax.dynamic_update_slice_in_dim(partial_value, product, first_slot, 0)

    rounds = (live_count + per_round - 1) // per_round
    return lax.fori_loop(0, rounds, one_round, jnp.zeros((total_slots, edge, edge), jnp.float32))


def on_device(x_tiles, x_cols, c_list, c_count):
    slot_pairs = c_list[0, 0]
    live_count = c_count[0, 0]
    partial_value = None
    for section_index in range(x_tiles.shape[0]):
        a_tiles, a_cols = (
            lax.all_gather(x_tiles[section_index], "col", axis=0, tiled=True),
            lax.all_gather(x_cols[section_index], "col", axis=0, tiled=True),
        )
        b_tiles, b_cols = (
            lax.all_gather(x_tiles[section_index], "row", axis=0, tiled=True),
            lax.all_gather(x_cols[section_index], "row", axis=0, tiled=True),
        )
        term = accumulate(
            a_tiles[None], a_cols[None], b_tiles[None], b_cols[None], slot_pairs, live_count
        )
        partial_value = term if partial_value is None else partial_value + term
    shares = lax.psum_scatter(
        partial_value.astype(jnp.bfloat16), "layer", scatter_dimension=0, tiled=True
    ).astype(jnp.float32)
    return shares[None, None]


def solution(mesh):
    return jax.shard_map(
        on_device,
        mesh=mesh,
        in_specs=(
            P("layer", ("row", "col"), None, None, None),
            P("layer", ("row", "col"), None),
            P("row", "col", None, None),
            P("row", "col"),
        ),
        out_specs=P("row", "col", "layer", None, None),
        check_vma=False,
    )
```

profile of v0, /device:TPU:1, one launch (start us, length us, event | category | flops | bytes accessed | tf_op | source)
XLA Modules:
  0.0 414.1 jit_solution(1684097884327743111)
XLA Ops:
  6.5 1.9 slice_bitcast_fusion
  8.5 0.7 all-gather.13.cloned.1.call-update
  9.2 0.7 all-gather.19.cloned.1.call-update
  11.4 22.2 %all-gather.5 = s32[1,64,2]{2,0,1:T(1,128)S(1)} all-gather(s32[1,4,2]{2,0,1:T(1,128)S(1)} %copy.70), channel_id=7, replica_groups=mesh['row'=4,'col'=16,'layer'=4] {'col'}, dimensions={1}, use_global_device_ids=true | all-gather | bytes 544 | tf_op jit(solution)/shard_map/all_gather | solution.py:46
  33.6 14.4 %all-gather.6 = s32[1,16,2]{2,0,1:T(1,128)S(1)} all-gather(s32[1,4,2]{2,0,1:T(1,128)S(1)} %copy.70), channel_id=8, replica_groups=mesh['row'=4,'col'=16,'layer'=4] {'row'}, dimensions={1}, use_global_device_ids=true | all-gather | bytes 160 | tf_op jit(solution)/shard_map/all_gather | solution.py:50
  48.0 10.5 %all-gather.2 = s32[1,16,2]{2,0,1:T(1,128)S(1)} all-gather(s32[1,4,2]{2,0,1:T(1,128)S(1)} %copy.68), channel_id=4, replica_groups=mesh['row'=4,'col'=16,'layer'=4] {'row'}, dimensions={1}, use_global_device_ids=true | all-gather | bytes 160 | tf_op jit(solution)/shard_map/all_gather | solution.py:50
  58.5 20.5 %all-gather.1 = s32[1,64,2]{2,0,1:T(1,128)S(1)} all-gather(s32[1,4,2]{2,0,1:T(1,128)S(1)} %copy.68), channel_id=3, replica_groups=mesh['row'=4,'col'=16,'layer'=4] {'col'}, dimensions={1}, use_global_device_ids=true | all-gather | bytes 544 | tf_op jit(solution)/shard_map/all_gather | solution.py:46
  79.4 9.0 %all-gather.13.cloned.1.call-done = bf16[1,64,2,128,128]{4,3,2,0,1:T(8,128)(2,1)} async-done(((bf16[1,4,2,128,128]{4,3,2,0,1:T(8,128)(2,1)}), bf16[1,64,2,128,128]{4,3,2,0,1:T(8,128)(2,1)}) %all-gather.13.cloned.1.call-update) | async-done | bytes 4194320 | tf_op jit(solution)/shard_map/all_gather | solution.py:45
  88.4 7.9 %broadcast.232.clone = f32[256,128,128]{2,1,0:T(8,128)} broadcast(f32[]{:T(128)} %constant.125.clone.1), dimensions={} | broadcast | bytes 16777220 | tf_op jit(solution)/shard_map/broadcast.1
  96.3 50.3 %while.24 = (s32[]{:T(128)}, f32[256,128,128]{2,1,0:T(8,128)}, s32[]{:T(128)}, s32[]{:T(128)}, s32[256,2]{0,1:T(2,128)S(1)}, /*index=5*/bf16[1,64,2,128,128]{4,3...) while((s32[]{:T(128)}, f32[256,128,128]{2,1,0:T(8,128)}, ...), condition=%wide.region_2.7_spmd, body=%wide.region_0.6_spmd.sunk | while | flops 274205376 | bytes 31473880 | solution.py:36
  98.8 4.3 %gather_fusion.3 = bf16[32,2,128,128]{3,2,1,0:T(8,128)(2,1)} fusion(bf16[64,2,128,128]{3,2,1,0:T(8,128)(2,1)} %bitcast.169, s32[1024]{0:T(1024)S(1)} %get-tuple-element.454), kind=kCustom, calls=%fused_computation.clone.clone.1 | custom fusion | bytes 4194432 | tf_op jit(solution)/shard_map/while/body/jit(_take)/gather | solution.py:17
  103.1 0.9 gather_fusion.2
  104.4 2.3 select_reduce_fusion.4
  106.7 2.1 fusion.42
  111.4 4.4 %gather_fusion.3 = bf16[32,2,128,128]{3,2,1,0:T(8,128)(2,1)} fusion(bf16[64,2,128,128]{3,2,1,0:T(8,128)(2,1)} %bitcast.169, s32[1024]{0:T(1024)S(1)} %get-tuple-element.454), kind=kCustom, calls=%fused_computation.clone.clone.1 | custom fusion | bytes 4194432 | tf_op jit(solution)/shard_map/while/body/jit(_take)/gather | solution.py:17
  115.7 0.9 gather_fusion.2
  117.0 2.3 select_reduce_fusion.4
  119.3 2.1 fusion.42
  124.0 4.3 %gather_fusion.3 = bf16[32,2,128,128]{3,2,1,0:T(8,128)(2,1)} fusion(bf16[64,2,128,128]{3,2,1,0:T(8,128)(2,1)} %bitcast.169, s32[1024]{0:T(1024)S(1)} %get-tuple-element.454), kind=kCustom, calls=%fused_computation.clone.clone.1 | custom fusion | bytes 4194432 | tf_op jit(solution)/shard_map/while/body/jit(_take)/gather | solution.py:17
  128.3 0.9 gather_fusion.2
  129.5 2.3 select_reduce_fusion.4
  131.9 2.1 fusion.42
  136.5 4.3 %gather_fusion.3 = bf16[32,2,128,128]{3,2,1,0:T(8,128)(2,1)} fusion(bf16[64,2,128,128]{3,2,1,0:T(8,128)(2,1)} %bitcast.169, s32[1024]{0:T(1024)S(1)} %get-tuple-element.454), kind=kCustom, calls=%fused_computation.clone.clone.1 | custom fusion | bytes 4194432 | tf_op jit(solution)/shard_map/while/body/jit(_take)/gather | solution.py:17
  140.9 0.9 gather_fusion.2
  142.1 2.3 select_reduce_fusion.4
  144.4 2.1 fusion.42
  146.6 18.8 %all-gather.17.cloned.1.call-done = bf16[1,64,2,128,128]{4,3,2,0,1:T(8,128)(2,1)} async-done(((bf16[1,4,2,128,128]{4,3,2,0,1:T(8,128)(2,1)}), bf16[1,64,2,128,128]{4,3,2,0,1:T(8,128)(2,1)}) %all-gather.17.cloned.1.call-update) | async-done | bytes 4194320 | tf_op jit(solution)/shard_map/all_gather | solution.py:45
  165.4 7.9 %broadcast.232.clone.1 = f32[256,128,128]{2,1,0:T(8,128)} broadcast(f32[]{:T(128)} %constant.125.clone.1), dimensions={} | broadcast | bytes 16777220 | tf_op jit(solution)/shard_map/broadcast.1
  173.2 50.3 %while.25 = (s32[]{:T(128)}, f32[256,128,128]{2,1,0:T(8,128)}, s32[]{:T(128)}, s32[]{:T(128)}, s32[256,2]{0,1:T(2,128)S(1)}, /*index=5*/bf16[1,64,2,128,128]{4,3...) while((s32[]{:T(128)}, f32[256,128,128]{2,1,0:T(8,128)}, ...), condition=%wide.region_5.10_spmd, body=%wide.region_3.9_spmd.sunk | while | flops 274205376 | bytes 31473880 | solution.py:36
  175.8 4.3 %gather_fusion.7 = bf16[32,2,128,128]{3,2,1,0:T(8,128)(2,1)} fusion(bf16[64,2,128,128]{3,2,1,0:T(8,128)(2,1)} %bitcast.167, s32[1024]{0:T(1024)S(1)} %get-tuple-element.469), kind=kCustom, calls=%fused_computation.4.clone.clone.1 | custom fusion | bytes 4194432 | tf_op jit(solution)/shard_map/while/body/jit(_take)/gather | solution.py:17
  180.1 0.9 gather_fusion.6
  181.4 2.3 select_reduce_fusion.5
  183.7 2.1 fusion.48
  188.4 4.3 %gather_fusion.7 = bf16[32,2,128,128]{3,2,1,0:T(8,128)(2,1)} fusion(bf16[64,2,128,128]{3,2,1,0:T(8,128)(2,1)} %bitcast.167, s32[1024]{0:T(1024)S(1)} %get-tuple-element.469), kind=kCustom, calls=%fused_computation.4.clone.clone.1 | custom fusion | bytes 4194432 | tf_op jit(solution)/shard_map/while/body/jit(_take)/gather | solution.py:17
  192.7 0.9 gather_fusion.6
  193.9 2.3 select_reduce_fusion.5
  196.3 2.1 fusion.48
  200.9 4.3 %gather_fusion.7 = bf16[32,2,128,128]{3,2,1,0:T(8,128)(2,1)} fusion(bf16[64,2,128,128]{3,2,1,0:T(8,128)(2,1)} %bitcast.167, s32[1024]{0:T(1024)S(1)} %get-tuple-element.469), kind=kCustom, calls=%fused_computation.4.clone.clone.1 | custom fusion | bytes 4194432 | tf_op jit(solution)/shard_map/while/body/jit(_take)/gather | solution.py:17
  205.2 0.9 gather_fusion.6
  206.5 2.3 select_reduce_fusion.5
  208.8 2.1 fusion.48
  213.5 4.3 %gather_fusion.7 = bf16[32,2,128,128]{3,2,1,0:T(8,128)(2,1)} fusion(bf16[64,2,128,128]{3,2,1,0:T(8,128)(2,1)} %bitcast.167, s32[1024]{0:T(1024)S(1)} %get-tuple-element.469), kind=kCustom, calls=%fused_computation.4.clone.clone.1 | custom fusion | bytes 4194432 | tf_op jit(solution)/shard_map/while/body/jit(_take)/gather | solution.py:17
  217.8 0.9 gather_fusion.6
  219.1 2.3 select_reduce_fusion.5
  221.4 2.1 fusion.48
  223.5 15.2 %add_convert_fusion = bf16[256,128,128]{2,1,0:T(8,128)(2,1)} fusion(f32[256,128,128]{2,1,0:T(8,128)} %get-tuple-element.241, f32[256,128,128]{2,1,0:T(8,128)} %get-tuple-element.242), kind=kLoop, calls=%fused_computation.56 | loop fusion | flops 8388608 | bytes 41943040 | tf_op jit(solution)/shard_map/convert_element_type | solution.py:57
  238.7 164.7 %reduce-scatter.2.cloned.1.call-done = bf16[64,128,128]{2,1,0:T(8,128)(2,1)} async-done(((bf16[256,128,128]{2,1,0:T(8,128)(2,1)}), bf16[64,128,128]{2,1,0:T(8,128)(2,1)}) %reduce-scatter.2.cloned.1.call-update) | async-done | bytes 2097168 | tf_op jit(solution)/shard_map/reduce_scatter | solution.py:56
  403.5 4.1 bitcast_convert_fusion
  (169 shorter events, 23.6 us)
Async XLA Ops:
  6.5 4.7 %copy-start.5 = (s32[2,4,2]{1,2,0:T(2,128)S(1)}, s32[2,4,2]{1,2,0:T(2,128)}, u32[]{:S(2)}) copy-start(s32[2,4,2]{1,2,0:T(2,128)} %param.17) | copy-start | bytes 196
  6.5 72.8 %all-gather.15.cloned.1.call-start = ((), (), s32[]{:S(2)}) async-start(), calls=%async_computation.3 | async-start | bytes 1310720 | tf_op jit(solution)/shard_map/all_gather | solution.py:49
  8.4 79.9 %all-gather.13.cloned.1.call-start = ((), (), s32[]{:S(2)}) async-start(), calls=%async_computation.2 | async-start | bytes 4456448 | tf_op jit(solution)/shard_map/all_gather | solution.py:45
  9.2 137.4 %all-gather.19.cloned.1.call-start = ((), (), s32[]{:S(2)}) async-start(), calls=%async_computation.5 | async-start | bytes 1310720 | tf_op jit(solution)/shard_map/all_gather | solution.py:49
  9.9 155.4 %all-gather.17.cloned.1.call-start = ((), (), s32[]{:S(2)}) async-start(), calls=%async_computation.4 | async-start | bytes 4456448 | tf_op jit(solution)/shard_map/all_gather | solution.py:45
  10.5 393.0 %reduce-scatter.2.cloned.1.call-start = ((), (), s32[]{:S(2)}) async-start(), calls=%async_computation.1 | async-start | bytes 10485760 | tf_op jit(solution)/shard_map/reduce_scatter | solution.py:56
  88.4 7.9 %copy-start.1 = (bf16[1,16,2,128,128]{4,3,2,0,1:T(8,128)(2,1)S(1)}, bf16[1,16,2,128,128]{4,3,2,0,1:T(8,128)(2,1)}, u32[]{:S(2)}) copy-start(bf16[1,16,2,128,128]{4,3,2,0,1:T(8,128)(2,1)} %all-gather.15.cloned.1.call-done) | copy-start | bytes 3145732
  88.4 7.9 %copy-start.4 = (s32[1,1,256,2]{2,3,1,0:T(2,128)S(1)}, s32[1,1,256,2]{2,3,1,0:T(2,128)}, u32[]{:S(2)}) copy-start(s32[1,1,256,2]{2,3,1,0:T(2,128)} %param.18) | copy-start | bytes 6148
  104.4 2.3 copy-start.2
  117.0 2.3 copy-start.2
  129.5 2.3 copy-start.2
  142.1 2.3 copy-start.2
  165.4 7.9 %copy-start = (bf16[1,16,2,128,128]{4,3,2,0,1:T(8,128)(2,1)S(1)}, bf16[1,16,2,128,128]{4,3,2,0,1:T(8,128)(2,1)}, u32[]{:S(2)}) copy-start(bf16[1,16,2,128,128]{4,3,2,0,1:T(8,128)(2,1)} %all-gather.19.cloned.1.call-done) | copy-start | bytes 3145732
  181.4 2.3 copy-start.3
  193.9 2.3 copy-start.3
  206.5 2.3 copy-start.3
  219.0 2.3 copy-start.3
Sparse Core Ops, SparseCore 0:
  9.2 38.8 all-gather.14
  50.0 38.3 all-gather.12
  90.2 34.3 all-gather.18
  126.3 38.9 all-gather.16
  238.9 164.5 reduce-scatter.1
where the time goes:
time: 415 us; the launch traced here: 414 us
  waiting for transfers between devices  194 us (47%)
  local copies, waits for them, and re-layouts  74.3 us (18%)
  blocking collectives  67.6 us (16%)
  other arithmetic  46.3 us (11%)
  matrix products  16.9 us (4%)
  between operations  13.8 us (3%)
    reduce_scatter x1, waiting for transfers between devices, on_device(): lax.psum_scatter(partial_value.astype(jnp.bfloat16), 'layer', scatter_dim...  165 us
    all_gather x2, blocking collectives, on_device(): lax.all_gather(x_cols[section_index], 'col', axis=0, tiled=True)  42.7 us
    gather x8, local copies, waits for them, and re-layouts, one_round(): left_tiles = jnp.take(a_tiles, chosen_rows[:, 0], axis=1)  34.6 us
    all_gather x2, waiting for transfers between devices, on_device(): lax.all_gather(x_tiles[section_index], 'col', axis=0, tiled=True)  27.8 us
    all_gather x2, blocking collectives, on_device(): lax.all_gather(x_cols[section_index], 'row', axis=0, tiled=True)  24.9 us
    reduce_sum x8, other arithmetic, one_round(): jnp.sum(jnp.where(matches[..., None, None], right_tiles[:, :, None], jnp....  18.5 us
    dot_general x8, matrix products, one_round(): jnp.einsum('sgpik,sgpjk->gij', left_tiles, picked, preferred_element_type...  16.9 us
    another operation x2, local copies, waits for them, and re-layouts  15.7 us
  transfers between devices with their start and end apart: 5, of which 3 were waited for; matrix products, arithmetic and copies ran while one was open for 14% of the time, Pallas kernels for 0%

commit v1 on v0

v1 whole, which is shorter than its diff:
```python
import jax
import jax.numpy as jnp
from jax import lax
from jax.experimental import pallas as pl
from jax.experimental.pallas import tpu as pltpu
from jax.sharding import PartitionSpec as P

EDGE = 128
CHUNK = 8
ZERO = 64
MESH = pl.DeviceIdType.MESH


def kernel(
    x_ref, xc_ref, cl_ref, cnt_ref, out_ref,
    a, b, fs, fr, ns, nr, own, ca, cb, crow, csm, idx,
    loc, gsend, a_recv, b_recv, csend, ca_recv, cb_recv, cl_sem,
    f_send, f_recv, n_send, n_recv, o_sem,
):
    row, col, lay = lax.axis_index("row"), lax.axis_index("col"), lax.axis_index("layer")
    zl, y, core = col // 8, (col // 2) % 4, col % 2
    pcol = (col + 8) % 16
    dz = 2 * zl - 1

    def col_of(z, yy):
        return (z * 4 + yy) * 2 + core

    rp, rm, rf = (row + 1) % 4, (row + 3) % 4, (row + 2) % 4
    rd = (row + 4 + dz) % 4
    re = (row + 4 - dz) % 4
    yp, ym, yf = (y + 1) % 4, (y + 3) % 4, (y + 2) % 4
    lp, lm, lf = (lay + 1) % 4, (lay + 3) % 4, (lay + 2) % 4
    sib = col + 1 - 2 * core
    zp = 1 - zl

    here = pl.ds(0, 8)
    my = [pltpu.make_async_copy(x_ref, a.at[pl.ds(col * 16, 16)], loc.at[0]),
          pltpu.make_async_copy(x_ref, b.at[pl.ds(row * 16, 16)], loc.at[1])]
    for m in my:
        m.start()

    barrier = pltpu.get_barrier_semaphore()
    peers = []
    for k in range(1, 8):
        peers.append((row, ((col // 2 + k) % 8) * 2 + core, lay))
    for r in (rp, rm, rf):
        peers.append((r, col, lay))
    peers += [(row, sib, lay), (rd, pcol, lay), (row, col, lp), (row, col, lm)]
    for p in peers:
        pl.semaphore_signal(barrier, inc=1, device_id=p, device_id_type=MESH)

    lane = lax.broadcasted_iota(jnp.int32, (8, EDGE), 1)
    vals = jnp.zeros((8, EDGE), jnp.int32)
    for s in range(2):
        for k in range(4):
            for p in range(2):
                vals = jnp.where(lane == s * 8 + k * 2 + p, xc_ref[s, p, k], vals)
    cidx = zl * 4 + y
    ca[core, cidx] = vals
    cb[row] = vals
    b[ZERO] = jnp.zeros((EDGE, EDGE), jnp.bfloat16)

    pl.semaphore_wait(barrier, len(peers))

    started = []

    def send(src, dst, ssem, rsem, dev):
        d = pltpu.make_async_remote_copy(
            src_ref=src, dst_ref=dst, send_sem=ssem, recv_sem=rsem,
            device_id=dev, device_id_type=MESH)
        d.start()
        started.append(d)

    n = 0
    for k in range(1, 8):
        send(ca.at[core, cidx], ca.at[core, cidx], csend.at[n], ca_recv.at[cidx],
             (row, ((col // 2 + k) % 8) * 2 + core, lay))
        n += 1
    for r in (rp, rm, rf):
        send(cb.at[row], cb.at[row], csend.at[n], cb_recv.at[row], (r, col, lay))
        n += 1

    count = [0]

    def send_a(c, s, dev):
        part = a.at[pl.ds(c * 16 + s * 8, 8)]
        send(part, part, gsend.at[count[0]], a_recv.at[c, s], dev)
        count[0] += 1

    def send_b(r, s, dev):
        part = b.at[pl.ds(r * 16 + s * 8, 8)]
        send(part, part, gsend.at[count[0]], b_recv.at[r, s], dev)
        count[0] += 1

    def wait_a(c, s):
        part = a.at[pl.ds(c * 16 + s * 8, 8)]
        pltpu.make_async_remote_copy(
            src_ref=part, dst_ref=part, send_sem=gsend.at[0], recv_sem=a_recv.at[c, s],
            device_id=(row, sib, lay), device_id_type=MESH).wait_recv()

    def wait_b(r, s):
        part = b.at[pl.ds(r * 16 + s * 8, 8)]
        pltpu.make_async_remote_copy(
            src_ref=part, dst_ref=part, send_sem=gsend.at[0], recv_sem=b_recv.at[r, s],
            device_id=(row, sib, lay), device_id_type=MESH).wait_recv()

    to_p = (row, pcol, lay)
    to_yp, to_ym = (row, col_of(zl, yp), lay), (row, col_of(zl, ym), lay)
    to_sib = (row, sib, lay)
    to_d, to_pd = (rd, col, lay), (rd, pcol, lay)
    to_rp, to_rm = (rp, col, lay), (rm, col, lay)

    for m in my:
        m.wait()

    send_a(col, zl, to_p)
    send_a(col, 0, to_yp)
    send_a(col, 1, to_ym)
    send_a(col, zp, to_p)
    send_a(col, 1, to_yp)
    send_a(col, 0, to_ym)
    send_b(row, zp, to_d)
    send_b(row, zl, to_d)
    send_a(col, 0, to_sib)
    send_a(col, 1, to_sib)

    def pass_p(s):
        wait_a(pcol, s)
        send_a(pcol, s, to_yp)
        send_a(pcol, s, to_ym)
        part = a.at[pl.ds(pcol * 16 + s * 8, 8)]
        send(part, b.at[pl.ds(row * 16 + s * 8, 8)], gsend.at[count[0]],
             b_recv.at[row, s], to_pd)
        count[0] += 1
        send_a(pcol, s, to_sib)

    def pass_y(z):
        cm, cp = col_of(z, ym), col_of(z, yp)
        wait_a(cm, 0)
        send_a(cm, 0, to_yp)
        wait_a(cp, 1)
        send_a(cp, 1, to_ym)
        send_a(cm, 0, to_sib)
        send_a(cp, 1, to_sib)

    def rest_y(z):
        cm, cp = col_of(z, ym), col_of(z, yp)
        wait_a(cm, 1)
        send_a(cm, 1, to_sib)
        wait_a(cp, 0)
        send_a(cp, 0, to_sib)

    def far_y(z):
        cf = col_of(z, yf)
        for s in range(2):
            wait_a(cf, s)
            send_a(cf, s, to_sib)

    pass_p(zp)
    pass_y(zl)
    wait_b(re, zp)
    send_b(re, zp, to_d)
    pass_p(zl)
    rest_y(zl)
    wait_b(rd, zl)
    send_b(rd, zl, (re, col, lay))
    pass_y(zp)

    for k in range(1, 8):
        ci = (cidx + k) % 8
        pltpu.make_async_remote_copy(
            src_ref=ca.at[core, ci], dst_ref=ca.at[core, ci], send_sem=csend.at[0],
            recv_sem=ca_recv.at[ci], device_id=to_sib, device_id_type=MESH).wait_recv()
    send(ca.at[core], ca.at[core], csend.at[n], ca_recv.at[8], to_sib)
    for r in (rp, rm, rf):
        pltpu.make_async_remote_copy(
            src_ref=cb.at[r], dst_ref=cb.at[r], send_sem=csend.at[0],
            recv_sem=cb_recv.at[r], device_id=to_sib, device_id_type=MESH).wait_recv()
    pltpu.make_async_remote_copy(
        src_ref=ca.at[1 - core], dst_ref=ca.at[1 - core], send_sem=csend.at[0],
        recv_sem=ca_recv.at[8], device_id=to_sib, device_id_type=MESH).wait_recv()
    for c in range(16):
        crow[c : c + 1, :] = ca[c % 2, c // 2, 0:1, :]
    for r in range(4):
        crow[16 + r : 17 + r, :] = cb[r, 0:1, :]
    for r in range(4):
        crow[20 + r : 21 + r, :] = jnp.zeros((1, EDGE), jnp.int32)
    to_smem = pltpu.make_async_copy(crow, csm, cl_sem)
    to_smem.start()
    to_smem.wait()
    live = cnt_ref[0, 0]

    def prepare(t, carry):
        av, bv = cl_ref[0, t], cl_ref[1, t]
        ah, al = av >> 2, (av & 3) * 2
        bh, bl = bv >> 2, (bv & 3) * 2
        idx[0, t] = ah * 16 + al
        alive = t < live
        for s in range(2):
            base = bh * 16 + s * 8 + bl
            q0, q1 = csm[16 + bh, s * 8 + bl], csm[16 + bh, s * 8 + bl + 1]
            for p in range(2):
                have = csm[ah, s * 8 + al + p]
                at = jnp.where(have == q0, base, jnp.where(have == q1, base + 1, ZERO))
                idx[1 + s * 2 + p, t] = jnp.where(alive, at, ZERO)
        return carry

    lax.fori_loop(0, 256, prepare, 0)

    rest_y(zp)
    far_y(zl)
    far_y(zp)
    for z in range(2):
        for yy in range(4):
            c = (z * 4 + yy) * 2 + 1 - core
            wait_a(c, 0)
            wait_a(c, 1)
    wait_b(re, zl)
    wait_b(rd, zp)
    wait_b(rf, 0)
    wait_b(rf, 1)

    def product(t):
        ai = idx[0, t]
        left = jnp.concatenate([a[ai], a[ai + 1], a[ai + 8], a[ai + 9]], axis=1)
        right = jnp.concatenate([b[idx[1 + q, t]] for q in range(4)], axis=1)
        return lax.dot_general(left, right, (((1,), (1,)), ((), ())),
                               preferred_element_type=jnp.float32)

    def rs_copy(src, dst, ssem, rsem, dev):
        return pltpu.make_async_remote_copy(
            src_ref=src, dst_ref=dst, send_sem=ssem, recv_sem=rsem,
            device_id=dev, device_id_type=MESH)

    ring = [(row, col, lp), (row, col, lm)]
    UNROLL = 4

    def slots(body):
        def step(i, carry):
            for u in range(UNROLL):
                body(i * UNROLL + u)
            return carry
        lax.fori_loop(0, CHUNK // UNROLL, step, 0)

    def f_copy(d, k):
        part = pl.ds(k * CHUNK, CHUNK)
        return rs_copy(fs.at[d, part], fr.at[d, part], f_send.at[d, k], f_recv.at[d, k], ring[d])

    def n_copy(d, k):
        part = pl.ds(k * CHUNK, CHUNK)
        return rs_copy(ns.at[d, part], nr.at[d, part], n_send.at[d, k], n_recv.at[d, k], ring[d])

    KH = 32 // CHUNK

    def far(k, carry):
        for d in range(2):
            base = lf * 64 + d * 32 + k * CHUNK
            slots(lambda i: fs.__setitem__((d, k * CHUNK + i), product(base + i).astype(jnp.bfloat16)))
            f_copy(d, k).start()
        return carry

    lax.fori_loop(0, KH, far, 0)

    def near(k, carry):
        for d, owner in ((0, lp), (1, lm)):
            at = (1 - d) * 32 + k * CHUNK
            base = owner * 64 + at
            slots(lambda i: ns.__setitem__((d, at + i), product(base + i).astype(jnp.bfloat16)))
            n_copy(d, (1 - d) * KH + k).start()
        return carry

    lax.fori_loop(0, KH, near, 0)

    def both(k, carry):
        for d, owner in ((0, lp), (1, lm)):
            at = d * 32 + k * CHUNK
            base = owner * 64 + at
            f_copy(d, k).wait_recv()
            slots(lambda i: ns.__setitem__(
                (d, at + i),
                (product(base + i) + fr[d, k * CHUNK + i].astype(jnp.float32)).astype(jnp.bfloat16)))
            n_copy(d, d * KH + k).start()
        return carry

    lax.fori_loop(0, KH, both, 0)

    def mine(k, carry):
        base = lay * 64 + k * CHUNK
        slots(lambda i: own.__setitem__(k * CHUNK + i, product(base + i)))
        return carry

    lax.fori_loop(0, 2 * KH, mine, 0)

    def o_copy(k):
        part = pl.ds(k * CHUNK, CHUNK)
        return pltpu.make_async_copy(own.at[part], out_ref.at[part], o_sem.at[k])

    def finish(k, carry):
        for d in range(2):
            at = d * KH + k
            n_copy(1 - d, at).wait_recv()
            n_copy(d, at).wait_recv()
            part = pl.ds(at * CHUNK, CHUNK)
            own[part] = own[part] + (nr[0, part].astype(jnp.float32) + nr[1, part].astype(jnp.float32))
            o_copy(at).start()
        return carry

    lax.fori_loop(0, KH, finish, 0)

    for d in started:
        d.wait_send()
    for d in range(2):
        lax.fori_loop(0, KH, lambda k, c: (f_copy(d, k).wait_send(), c)[1], 0)
        lax.fori_loop(0, 2 * KH, lambda k, c: (n_copy(d, k).wait_send(), c)[1], 0)
    lax.fori_loop(0, 2 * KH, lambda k, c: (o_copy(k).wait(), c)[1], 0)


def on_device(x_tiles, x_cols, c_list, c_count):
    hbm, smem = pl.BlockSpec(memory_space=pl.ANY), pl.BlockSpec(memory_space=pltpu.SMEM)
    tile = (EDGE, EDGE)
    dma = pltpu.SemaphoreType.DMA
    out = pl.pallas_call(
        kernel,
        out_shape=jax.ShapeDtypeStruct((64,) + tile, jnp.float32),
        in_specs=[hbm, smem, smem, smem],
        out_specs=hbm,
        scratch_shapes=[
            pltpu.VMEM((256,) + tile, jnp.bfloat16),
            pltpu.VMEM((65,) + tile, jnp.bfloat16),
            pltpu.VMEM((2, 32) + tile, jnp.bfloat16),
            pltpu.VMEM((2, 32) + tile, jnp.bfloat16),
            pltpu.VMEM((2, 64) + tile, jnp.bfloat16),
            pltpu.VMEM((2, 64) + tile, jnp.bfloat16),
            pltpu.VMEM((64,) + tile, jnp.float32),
            pltpu.VMEM((2, 8, 8, EDGE), jnp.int32),
            pltpu.VMEM((4, 8, EDGE), jnp.int32),
            pltpu.VMEM((24, EDGE), jnp.int32),
            pltpu.SMEM((24, EDGE), jnp.int32),
            pltpu.SMEM((8, 256), jnp.int32),
            dma((2,)), dma((48,)), dma((16, 2)), dma((4, 2)),
            dma((11,)), dma((9,)), dma((4,)), dma,
            dma((2, 32 // CHUNK)), dma((2, 32 // CHUNK)),
            dma((2, 64 // CHUNK)), dma((2, 64 // CHUNK)), dma((64 // CHUNK,)),
        ],
        compiler_params=pltpu.CompilerParams(
            collective_id=0, has_side_effects=True, vmem_limit_bytes=52 * 1024 * 1024),
    )(x_tiles.reshape((16,) + tile), jnp.swapaxes(x_cols, 1, 2),
      jnp.swapaxes(c_list[0, 0], 0, 1), c_count)
    return out[None, None]


def solution(mesh):
    return jax.shard_map(
        on_device,
        mesh=mesh,
        in_specs=(
            P("layer", ("row", "col"), None, None, None),
            P("layer", ("row", "col"), None),
            P("row", "col", None, None),
            P("row", "col"),
        ),
        out_specs=P("row", "col", "layer", None, None),
        check_vma=False,
    )
```

time: 415 us -> 142 us (0.34)
  waiting for transfers between devices: 194 us -> 0 us
  Pallas kernels: 0 us -> 134 us
  blocking collectives: 67.6 us -> 0 us
  local copies, waits for them, and re-layouts: 74.3 us -> 7.1 us
  other arithmetic: 46.3 us -> 0 us
  matrix products: 16.9 us -> 0 us
  between operations: 13.8 us -> 0.67 us
    reduce_scatter x1 -> x0, waiting for transfers between devices: 165 us -> none  [on_device(): lax.psum_scatter(partial_value.astype(jnp.bfloat16), 'layer', scatter_dim...]
    pallas_call x0 -> x1, Pallas kernels: none -> 134 us  [on_device(): pl.pallas_call(kernel, out_shape=jax.ShapeDtypeStruct((64,) + tile, jnp.f...]
    all_gather x4 -> x0, blocking collectives: 67.6 us -> none  [the longest x2 42.7 us: on_device(): lax.all_gather(x_cols[section_index], 'col', axis=0, tiled=True)]
    gather x48 -> x0, local copies, waits for them, and re-layouts: 52.7 us -> none  [the longest x8 34.6 us: one_round(): left_tiles = jnp.take(a_tiles, chosen_rows[:, 0], axis=1)]
    all_gather x4 -> x0, waiting for transfers between devices: 27.8 us -> none  [the longest x2 27.8 us: on_device(): lax.all_gather(x_tiles[section_index], 'col', axis=0, tiled=True)]
    reduce_sum x8 -> x0, other arithmetic: 18.5 us -> none  [one_round(): jnp.sum(jnp.where(matches[..., None, None], right_tiles[:, :, None], jnp....]
    another operation x18 -> x0, local copies, waits for them, and re-layouts: 17.2 us -> none
    dot_general x8 -> x0, matrix products: 16.9 us -> none  [one_round(): jnp.einsum('sgpik,sgpjk->gij', left_tiles, picked, preferred_element_type...]
  transfers between devices with their start and end apart: 5 -> 0, of which waited for: 3 -> 0; matrix products, arithmetic and copies ran while one was open for 14% -> 0% of each run, Pallas kernels for 0% -> 0%
where the time goes in v1:
time: 142 us; the launch traced here: 141 us
  Pallas kernels  134 us (94%)
  local copies, waits for them, and re-layouts  7.1 us (5%)
    pallas_call x1, Pallas kernels, on_device(): pl.pallas_call(kernel, out_shape=jax.ShapeDtypeStruct((64,) + tile, jnp.f...  134 us
    unnamed x7, local copies, waits for them, and re-layouts  7.1 us

profile of v1, /device:TPU:1, one launch (start us, length us, event | category | flops | bytes accessed | tf_op | source)
XLA Modules:
  0.0 141.4 jit_solution(4127353115799816466)
XLA Ops:
  0.7 0.0 copy-start
  0.7 1.0 copy-done
  1.7 0.0 copy-start.1
  1.7 0.7 copy-done.1
  2.4 0.0 copy-start.2
  2.4 0.7 copy-done.2
  3.1 133.6 %shard_map.46 = f32[64,128,128]{2,1,0:T(8,128)} custom-call(bf16[16,128,128]{2,1,0:T(8,128)(2,1)S(1)} %bitcast.6, s32[2,2,4]{2,1,0:T(2,128)S(1)} %bitcast.7, s32[2,256]{1,0:T(2,128)S(1)} %bitcast.8, s32[1,1]{1,0:T(1,128)S(6)} %copy.6.cnt_ref), custom_call_target="tpu_custom_call" | custom-call | tf_op jit(solution)/shard_map/pallas_call | solution.py:322
  136.7 4.7 %copy.7 = f32[1,1,64,128,128]{4,3,2,1,0:T(8,128)} copy(f32[1,1,64,128,128]{4,3,2,1,0:T(8,128)} %bitcast.9) | data formatting | bytes 8388608
Async XLA Ops:
  0.7 1.0 copy-start
  1.7 0.7 copy-start.1
  2.4 0.7 copy-start.2

commit v2 on v0

v2 whole, which is shorter than its diff:
```python
import jax
import jax.numpy as jnp
from jax import lax
from jax.experimental import pallas as pl
from jax.experimental.pallas import tpu as pltpu
from jax.sharding import PartitionSpec as P

EDGE = 128
HALF = 64
A_HALF = 256
B_HALF = 65
ZERO = 64
PAIRS = 16
Q_CHUNK = 8
R_CHUNK = 4
Q_PARTS = PAIRS // Q_CHUNK
R_PARTS = PAIRS // R_CHUNK
MESH = pl.DeviceIdType.MESH


def kernel(
    x_hbm, cols_hbm, list_hbm, count, out_ref,
    a0, a1, b0, b1, fq_out, fq_in, fr_out, fr_in, nq_out, nq_in, nr_out, nr_in,
    ca, cb, cols, pairs, idv, idx,
    loc, small, gsend, a_recv, b_recv, csend, ca_recv, cb_recv,
    fq_send, fq_recv, fr_send, fr_recv, nq_send, nq_recv, nr_send, nr_recv,
):
    row, col, lay = lax.axis_index("row"), lax.axis_index("col"), lax.axis_index("layer")
    zl, y, core = col // 8, (col // 2) % 4, col % 2
    zp = 1 - zl
    a, b = (a0, a1), (b0, b1)
    pcol = (col + 8) % 16
    sib = col + 1 - 2 * core
    dz = 2 * zl - 1
    cidx = zl * 4 + y

    def col_of(z, yy):
        return (z * 4 + yy) * 2 + core

    rp, rm, rf = (row + 1) % 4, (row + 3) % 4, (row + 2) % 4
    rd, re = (row + 4 + dz) % 4, (row + 4 - dz) % 4
    yp, ym, yf = (y + 1) % 4, (y + 3) % 4, (y + 2) % 4
    lp, lm, lf = (lay + 1) % 4, (lay + 3) % 4, (lay + 2) % 4

    def a_part(c, h, s):
        return a[h].at[pl.ds(c * 16 + s * 8, 8)]

    def b_part(r, h, s):
        return b[h].at[pl.ds(r * 16 + s * 8, 8)]

    cols_in = pltpu.make_async_copy(cols_hbm, cols, small.at[0])
    list_in = pltpu.make_async_copy(list_hbm, pairs, small.at[1])
    own_in = []
    for h in range(2):
        rows = x_hbm.at[:, pl.ds(h * HALF, HALF)]
        own_in.append((
            pltpu.make_async_copy(rows, a[h].at[pl.ds(col * 16, 16)], loc.at[h, 0]),
            pltpu.make_async_copy(rows, b[h].at[pl.ds(row * 16, 16)], loc.at[h, 1])))
    cols_in.start()
    for pair in own_in:
        for m in pair:
            m.start()
    list_in.start()

    barrier = pltpu.get_barrier_semaphore()
    chips = [(row, ((col // 2 + k) % 8) * 2 + core, lay) for k in range(1, 8)]
    ends = [(r, col, lay) for r in (rp, rm, rf)]
    peers = chips + ends + [(row, sib, lay), (rd, pcol, lay), (row, col, lp), (row, col, lm)]
    for p in peers:
        pl.semaphore_signal(barrier, inc=1, device_id=p, device_id_type=MESH)

    cols_in.wait()
    lane = lax.broadcasted_iota(jnp.int32, (8, EDGE), 1)
    sub = lax.broadcasted_iota(jnp.int32, (8, EDGE), 0)
    for first, where in ((col * 4, ca.at[core, cidx]), (row * 4, cb.at[row])):
        vals = jnp.zeros((8, EDGE), jnp.int32)
        for s in range(2):
            for k in range(4):
                for p in range(2):
                    vals = jnp.where((lane == first + k) & (sub == s * 2 + p), cols[s, p, k], vals)
        where[...] = vals
    for h in range(2):
        b[h][ZERO] = jnp.zeros((HALF, EDGE), jnp.bfloat16)

    pl.semaphore_wait(barrier, len(peers))

    started = []

    def copy_to(src, dst, ssem, rsem, dev):
        return pltpu.make_async_remote_copy(
            src_ref=src, dst_ref=dst, send_sem=ssem, recv_sem=rsem,
            device_id=dev, device_id_type=MESH)

    def send(src, dst, ssem, rsem, dev):
        d = copy_to(src, dst, ssem, rsem, dev)
        d.start()
        started.append(d)

    to_sib = (row, sib, lay)
    to_p, to_d, to_pd, to_e = (row, pcol, lay), (rd, col, lay), (rd, pcol, lay), (re, col, lay)
    to_yp, to_ym = (row, col_of(zl, yp), lay), (row, col_of(zl, ym), lay)

    for n, dev in enumerate(chips):
        send(ca.at[core, cidx], ca.at[core, cidx], csend.at[n], ca_recv.at[cidx], dev)
    for n, dev in enumerate(ends):
        send(cb.at[row], cb.at[row], csend.at[7 + n], cb_recv.at[row], dev)

    used = [0]

    def next_sem():
        used[0] += 1
        return gsend.at[used[0] - 1]

    def send_a(c, h, s, dev):
        send(a_part(c, h, s), a_part(c, h, s), next_sem(), a_recv.at[h, c, s], dev)

    def send_b(r, h, s, dev):
        send(b_part(r, h, s), b_part(r, h, s), next_sem(), b_recv.at[h, r, s], dev)

    def wait_a(c, h, s):
        copy_to(a_part(c, h, s), a_part(c, h, s), gsend.at[0], a_recv.at[h, c, s], to_sib).wait_recv()

    def wait_b(r, h, s):
        copy_to(b_part(r, h, s), b_part(r, h, s), gsend.at[0], b_recv.at[h, r, s], to_sib).wait_recv()

    def own_block(h):
        for m in own_in[h]:
            m.wait()
        send_a(col, h, zl, to_p)
        send_a(col, h, 0, to_yp)
        send_a(col, h, 1, to_ym)
        send_b(row, h, zp, to_d)
        send_a(col, h, zp, to_p)
        send_a(col, h, 1, to_yp)
        send_a(col, h, 0, to_ym)
        send_b(row, h, zl, to_d)
        send_a(col, h, 0, to_sib)
        send_a(col, h, 1, to_sib)

    def pass_p(h, s):
        wait_a(pcol, h, s)
        send_a(pcol, h, s, to_yp)
        send_a(pcol, h, s, to_ym)
        send(a_part(pcol, h, s), b_part(row, h, s), next_sem(), b_recv.at[h, row, s], to_pd)
        send_a(pcol, h, s, to_sib)

    def pass_y(h, z):
        cm, cp = col_of(z, ym), col_of(z, yp)
        wait_a(cm, h, 0)
        send_a(cm, h, 0, to_yp)
        wait_a(cp, h, 1)
        send_a(cp, h, 1, to_ym)
        send_a(cm, h, 0, to_sib)
        send_a(cp, h, 1, to_sib)

    def rest_y(h, z):
        cm, cp = col_of(z, ym), col_of(z, yp)
        wait_a(cm, h, 1)
        send_a(cm, h, 1, to_sib)
        wait_a(cp, h, 0)
        send_a(cp, h, 0, to_sib)

    def far_y(h, z):
        cf = col_of(z, yf)
        for s in range(2):
            wait_a(cf, h, s)
            send_a(cf, h, s, to_sib)

    def far_b(h, which):
        if which == 0:
            wait_b(re, h, zp)
            send_b(re, h, zp, to_d)
        else:
            wait_b(rd, h, zl)
            send_b(rd, h, zl, to_e)

    def last(h):
        for z in range(2):
            for yy in range(4):
                c = (z * 4 + yy) * 2 + 1 - core
                wait_a(c, h, 0)
                wait_a(c, h, 1)
        wait_b(re, h, zl)
        wait_b(rd, h, zp)
        wait_b(rf, h, 0)
        wait_b(rf, h, 1)

    own_block(0)
    pass_y(0, zl)
    pass_p(0, zp)
    far_b(0, 0)
    pass_p(0, zl)
    rest_y(0, zl)
    pass_y(0, zp)
    far_b(0, 1)
    own_block(1)

    for k in range(1, 8):
        ci = (cidx + k) % 8
        copy_to(ca.at[core, ci], ca.at[core, ci], csend.at[0], ca_recv.at[ci], to_sib).wait_recv()
    send(ca.at[core], ca.at[core], csend.at[10], ca_recv.at[8], to_sib)
    for r in (rp, rm, rf):
        copy_to(cb.at[r], cb.at[r], csend.at[0], cb_recv.at[r], to_sib).wait_recv()
    copy_to(ca.at[1 - core], ca.at[1 - core], csend.at[0], ca_recv.at[8], to_sib).wait_recv()
    list_in.wait()
    acols = jnp.sum(ca[...].reshape(16, 8, EDGE), axis=0)
    bcols = jnp.sum(cb[...], axis=0)
    live = count[0, 0]
    for g in range(2):
        part = slice(g * EDGE, (g + 1) * EDGE)
        av = jnp.broadcast_to(pairs[0:1, part], (8, EDGE))
        bv = jnp.broadcast_to(pairs[1:2, part], (8, EDGE))
        have = jnp.take_along_axis(acols, av, axis=1, mode="promise_in_bounds")
        want = jnp.take_along_axis(bcols, bv, axis=1, mode="promise_in_bounds")
        ra, rb = av[0:1], bv[0:1]
        idv[0:1, part] = (ra >> 2) * 16 + (ra & 3) * 2
        alive = (lane[0:1] + g * EDGE) < live
        for s in range(2):
            base = (rb >> 2) * 16 + s * 8 + (rb & 3) * 2
            w0, w1 = want[s * 2 : s * 2 + 1], want[s * 2 + 1 : s * 2 + 2]
            for p in range(2):
                q = s * 2 + p
                h0 = have[q : q + 1]
                at = jnp.where(h0 == w0, base, jnp.where(h0 == w1, base + 1, ZERO))
                idv[1 + q : 2 + q, part] = jnp.where(alive, at, ZERO)
    idv[5:8, :] = jnp.zeros((3, 256), jnp.int32)
    to_smem = pltpu.make_async_copy(idv, idx, small.at[2])
    to_smem.start()
    to_smem.wait()

    rest_y(0, zp)
    far_y(0, zl)
    far_y(0, zp)
    last(0)

    def left_of(t, h):
        u = idx[0, t]
        return jnp.concatenate([a[h][u], a[h][u + 1], a[h][u + 8], a[h][u + 9]], axis=1)

    def right_of(t, h):
        return jnp.concatenate([b[h][idx[1 + q, t]] for q in range(4)], axis=1)

    def times(left, right):
        return lax.dot_general(left, right, (((1,), (1,)), ((), ())),
                               preferred_element_type=jnp.float32)

    low = lax.broadcasted_iota(jnp.int32, (HALF, EDGE), 1) < HALF

    def quadrants(t):
        both = times(jnp.concatenate([left_of(t, 0), left_of(t + 1, 0)], axis=0),
                     jnp.concatenate([right_of(t, 0), right_of(t + 1, 0)], axis=0))
        return jnp.where(low, both[:HALF], both[HALF:])

    def whole(t):
        return times(jnp.concatenate([left_of(t, 0), left_of(t, 1)], axis=0),
                     jnp.concatenate([right_of(t, 0), right_of(t, 1)], axis=0))

    def rest(t):
        one, two = whole(t), whole(t + 1)
        mixed = jnp.where(low, pltpu.roll(two[:HALF], HALF, 1), one[:HALF])
        return mixed, one[HALF:], two[HALF:]

    ring = [(row, col, lp), (row, col, lm)]

    def fq(d, k):
        part = pl.ds(k * Q_CHUNK, Q_CHUNK)
        return copy_to(fq_out.at[d, part], fq_in.at[d, part], fq_send.at[d, k], fq_recv.at[d, k], ring[d])

    def fr(d, k):
        part = pl.ds(k * R_CHUNK, R_CHUNK)
        return copy_to(fr_out.at[d, part], fr_in.at[d, part], fr_send.at[d, k], fr_recv.at[d, k], ring[d])

    def nq(d, g, k):
        part = pl.ds(k * Q_CHUNK, Q_CHUNK)
        return copy_to(nq_out.at[d, g, part], nq_in.at[d, g, part], nq_send.at[d, g, k],
                       nq_recv.at[d, g, k], ring[d])

    def nr(d, g, k):
        part = pl.ds(k * R_CHUNK, R_CHUNK)
        return copy_to(nr_out.at[d, g, part], nr_in.at[d, g, part], nr_send.at[d, g, k],
                       nr_recv.at[d, g, k], ring[d])

    def each(n, body, unroll):
        def step(i, carry):
            for u in range(unroll):
                body(i * unroll + u)
            return carry
        lax.fori_loop(0, n // unroll, step, 0)

    def half(v):
        return v.astype(jnp.bfloat16)

    def wide(v):
        return v.astype(jnp.float32)

    next_owner = (lp, lm)

    def far_q(k):
        for d in range(2):
            def body(i):
                j = k * Q_CHUNK + i
                fq_out[d, j] = half(quadrants(lf * 64 + d * 32 + 2 * j))
            each(Q_CHUNK, body, 4)
            fq(d, k).start()

    def near_q(k):
        for d in range(2):
            g = 1 - d
            def body(i):
                j = k * Q_CHUNK + i
                nq_out[d, g, j] = half(quadrants(next_owner[d] * 64 + g * 32 + 2 * j))
            each(Q_CHUNK, body, 4)
            nq(d, g, k).start()

    def sum_q(k):
        for d in range(2):
            fq(d, k).wait_recv()
            def body(i):
                j = k * Q_CHUNK + i
                nq_out[d, d, j] = half(
                    quadrants(next_owner[d] * 64 + d * 32 + 2 * j) + wide(fq_in[d, j]))
            each(Q_CHUNK, body, 4)
            nq(d, d, k).start()

    def loop(n, body):
        def step(k, carry):
            body(k)
            return carry
        lax.fori_loop(0, n, step, 0)

    loop(Q_PARTS, far_q)
    pass_y(1, zl)
    pass_p(1, zp)
    loop(Q_PARTS, near_q)
    far_b(1, 0)
    pass_p(1, zl)
    rest_y(1, zl)
    loop(Q_PARTS, sum_q)
    pass_y(1, zp)
    far_b(1, 1)
    rest_y(1, zp)
    far_y(1, zl)
    far_y(1, zp)
    last(1)

    def far_r(k):
        for d in range(2):
            def body(i):
                j = k * R_CHUNK + i
                for n, v in enumerate(rest(lf * 64 + d * 32 + 2 * j)):
                    fr_out[d, j, n] = half(v)
            each(R_CHUNK, body, 2)
            fr(d, k).start()

    def near_r(k):
        for d in range(2):
            g = 1 - d
            def body(i):
                j = k * R_CHUNK + i
                for n, v in enumerate(rest(next_owner[d] * 64 + g * 32 + 2 * j)):
                    nr_out[d, g, j, n] = half(v)
            each(R_CHUNK, body, 2)
            nr(d, g, k).start()

    def sum_r(k):
        for d in range(2):
            fr(d, k).wait_recv()
            def body(i):
                j = k * R_CHUNK + i
                for n, v in enumerate(rest(next_owner[d] * 64 + d * 32 + 2 * j)):
                    nr_out[d, d, j, n] = half(v + wide(fr_in[d, j, n]))
            each(R_CHUNK, body, 2)
            nr(d, d, k).start()

    loop(R_PARTS, far_r)
    loop(R_PARTS, near_r)

    def mine(t):
        out_ref[t] = whole(lay * 64 + t)

    each(64, mine, 4)
    loop(R_PARTS, sum_r)

    for d in range(2):
        for g in range(2):
            loop(Q_PARTS, lambda k: nq(d, g, k).wait_recv())

    def finish(k):
        for g in range(2):
            for d in range(2):
                nr(d, g, k).wait_recv()

            def body(i):
                j = k * R_CHUNK + i
                t = g * 32 + 2 * j
                first = wide(nq_in[0, g, j]) + wide(nq_in[1, g, j])
                mixed, one, two = (wide(nr_in[0, g, j, n]) + wide(nr_in[1, g, j, n]) for n in range(3))
                upper, lower = pl.ds(0, HALF), pl.ds(HALF, HALF)
                out_ref[t, upper] += jnp.where(low, first, mixed)
                out_ref[t, lower] += one
                out_ref[t + 1, upper] += pltpu.roll(jnp.where(low, mixed, first), HALF, 1)
                out_ref[t + 1, lower] += two

            each(R_CHUNK, body, 2)

    loop(R_PARTS, finish)

    for d in started:
        d.wait_send()
    for d in range(2):
        loop(Q_PARTS, lambda k: fq(d, k).wait_send())
        loop(R_PARTS, lambda k: fr(d, k).wait_send())
        for g in range(2):
            loop(Q_PARTS, lambda k: nq(d, g, k).wait_send())
            loop(R_PARTS, lambda k: nr(d, g, k).wait_send())


def on_device(x_tiles, x_cols, c_list, c_count):
    hbm = pl.BlockSpec(memory_space=pltpu.HBM)
    unit = (HALF, EDGE)
    dma = pltpu.SemaphoreType.DMA
    bf16 = lambda *dims: pltpu.VMEM(dims + unit, jnp.bfloat16)
    ints = lambda *dims: pltpu.VMEM(dims, jnp.int32)
    operands = [
        pltpu.with_memory_space_constraint(v, pltpu.HBM)
        for v in (x_tiles.reshape(16, EDGE, EDGE), jnp.swapaxes(x_cols, 1, 2),
                  jnp.swapaxes(c_list[0, 0], 0, 1))
    ]
    out = pl.pallas_call(
        kernel,
        out_shape=pltpu.VMEM((64, EDGE, EDGE), jnp.float32),
        in_specs=[hbm] * 3 + [pl.BlockSpec(memory_space=pltpu.SMEM)],
        out_specs=pl.BlockSpec(memory_space=pltpu.VMEM),
        scratch_shapes=[
            bf16(A_HALF), bf16(A_HALF), bf16(B_HALF), bf16(B_HALF),
            bf16(2, PAIRS), bf16(2, PAIRS), bf16(2, PAIRS, 3), bf16(2, PAIRS, 3),
            bf16(2, 2, PAIRS), bf16(2, 2, PAIRS), bf16(2, 2, PAIRS, 3), bf16(2, 2, PAIRS, 3),
            ints(2, 8, 8, EDGE), ints(4, 8, EDGE),
            pltpu.SMEM((2, 2, 4), jnp.int32), ints(2, 256),
            ints(8, 256), pltpu.SMEM((8, 256), jnp.int32),
            dma((2, 2)), dma((3,)), dma((72,)), dma((2, 16, 2)), dma((2, 4, 2)),
            dma((11,)), dma((9,)), dma((4,)),
            dma((2, Q_PARTS)), dma((2, Q_PARTS)), dma((2, R_PARTS)), dma((2, R_PARTS)),
            dma((2, 2, Q_PARTS)), dma((2, 2, Q_PARTS)), dma((2, 2, R_PARTS)), dma((2, 2, R_PARTS)),
        ],
        compiler_params=pltpu.CompilerParams(
            collective_id=0, has_side_effects=True, vmem_limit_bytes=40 * 1024 * 1024),
    )(*operands, c_count)
    return out[None, None]


def solution(mesh):
    return jax.shard_map(
        on_device,
        mesh=mesh,
        in_specs=(
            P("layer", ("row", "col"), None, None, None),
            P("layer", ("row", "col"), None),
            P("row", "col", None, None),
            P("row", "col"),
        ),
        out_specs=P("row", "col", "layer", None, None),
        check_vma=False,
    )
```

time: 415 us -> 115 us (0.28)
  waiting for transfers between devices: 194 us -> 0 us
  Pallas kernels: 0 us -> 113 us
  local copies, waits for them, and re-layouts: 74.3 us -> 2.02 us
  blocking collectives: 67.6 us -> 0 us
  other arithmetic: 46.3 us -> 0 us
  matrix products: 16.9 us -> 0 us
  between operations: 13.8 us -> 0.66 us
    reduce_scatter x1 -> x0, waiting for transfers between devices: 165 us -> none  [on_device(): lax.psum_scatter(partial_value.astype(jnp.bfloat16), 'layer', scatter_dim...]
    pallas_call x0 -> x1, Pallas kernels: none -> 113 us  [on_device(): pl.pallas_call(kernel, out_shape=pltpu.VMEM((64, EDGE, EDGE), jnp.float32...]
    all_gather x4 -> x0, blocking collectives: 67.6 us -> none  [the longest x2 42.7 us: on_device(): lax.all_gather(x_cols[section_index], 'col', axis=0, tiled=True)]
    gather x48 -> x0, local copies, waits for them, and re-layouts: 52.7 us -> none  [the longest x8 34.6 us: one_round(): left_tiles = jnp.take(a_tiles, chosen_rows[:, 0], axis=1)]
    all_gather x4 -> x0, waiting for transfers between devices: 27.8 us -> none  [the longest x2 27.8 us: on_device(): lax.all_gather(x_tiles[section_index], 'col', axis=0, tiled=True)]
    reduce_sum x8 -> x0, other arithmetic: 18.5 us -> none  [one_round(): jnp.sum(jnp.where(matches[..., None, None], right_tiles[:, :, None], jnp....]
    another operation x18 -> x0, local copies, waits for them, and re-layouts: 17.2 us -> none
    dot_general x8 -> x0, matrix products: 16.9 us -> none  [one_round(): jnp.einsum('sgpik,sgpjk->gij', left_tiles, picked, preferred_element_type...]
  transfers between devices with their start and end apart: 5 -> 0, of which waited for: 3 -> 0; matrix products, arithmetic and copies ran while one was open for 14% -> 0% of each run, Pallas kernels for 0% -> 0%
where the time goes in v2:
time: 115 us
  Pallas kernels  113 us (98%)
  local copies, waits for them, and re-layouts  2.02 us (2%)
    pallas_call x1, Pallas kernels, on_device(): pl.pallas_call(kernel, out_shape=pltpu.VMEM((64, EDGE, EDGE), jnp.float32...  113 us

profile of v2, /device:TPU:1, one launch (start us, length us, event | category | flops | bytes accessed | tf_op | source)
XLA Modules:
  0.0 115.3 jit_solution(12395943690189735218)
XLA Ops:
  0.7 112.6 %shard_map.46 = f32[64,128,128]{2,1,0:T(8,128)S(1)} custom-call(bf16[16,128,128]{2,1,0:T(8,128)(2,1)} %bitcast.7, s32[2,2,4]{2,1,0:T(2,128)} %bitcast.8, s32[2,256]{1,0:T(2,128)} %bitcast.9, s32[1,1]{1,0:T(1,128)S(6)} %copy.7.count), custom_call_target="tpu_custom_call" | custom-call | tf_op jit(solution)/shard_map/pallas_call | solution.py:429
  113.3 2.0 %copy.6 = f32[1,1,64,128,128]{4,3,2,1,0:T(8,128)} copy(f32[1,1,64,128,128]{4,3,2,1,0:T(8,128)S(1)} %bitcast.6) | data formatting | bytes 8388608

commit v3 on v2

v3 whole, which is shorter than its diff:
```python
import jax
import jax.numpy as jnp
from jax import lax
from jax.experimental import pallas as pl
from jax.experimental.pallas import tpu as pltpu
from jax.sharding import PartitionSpec as P

EDGE = 128
HALF = 64
ROWS = (64, 32, 32)
FIRST = (0, 64, 96)
A_UNITS = 256
B_UNITS = 65
ZERO = 64
PAIRS = 16
Q_PARTS, S_PARTS, R_PARTS = 4, 2, 4
MESH = pl.DeviceIdType.MESH
ORDER = (
    "0in", "0zp1", "0zp2", "0y0", "0y1", "0sb", "0d1", "0cols", "0q1", "0p1", "0d2", "0lists",
    "0p2", "0r1", "0b1", "0places", "0q2", "1in", "1y0", "1y1", "1zp1", "1zp2", "0b0", "1d1",
    "1d2", "1sb", "0r2", "0f1", "0f2", "0lastA", "0lastB", "0list", "F0", "F1", "1q1", "1p1",
    "F2", "F3", "1p2", "N0", "N1", "1r1", "2in", "2y0", "2y1", "2zp1", "2zp2", "2sb", "1b1",
    "1b0", "1q2", "N2", "N3", "2d1", "2d2", "S0", "S1", "2q1", "2p1", "S2", "S3", "1r2", "1f1",
    "1f2", "1lastA", "2p2", "f0", "f1", "2r1", "n0", "n1", "2b1", "2b0", "2q2", "s0", "s1",
    "2r2", "2f1", "2f2", "2lastA", "1lastB", "2lastB", "R",
)


def kernel(
    x_hbm, cols_hbm, list_hbm, count, out_ref,
    a0, a1, a2, b0, b1, b2, q_refs, s_refs, r_refs, ca, cb, cols, pairs, idv, idx,
    loc, small, gsend, a_recv, b_recv, csend, ca_recv, cb_recv,
    q_sems, s_sems, r_sems,
):
    row, col, lay = lax.axis_index("row"), lax.axis_index("col"), lax.axis_index("layer")
    zl, y, core = col // 8, (col // 2) % 4, col % 2
    zp = 1 - zl
    a, b = (a0, a1, a2), (b0, b1, b2)
    pcol = (col + 8) % 16
    sib = col + 1 - 2 * core
    dz = 2 * zl - 1
    cidx = zl * 4 + y

    def col_of(z, yy):
        return (z * 4 + yy) * 2 + core

    rp, rm, rf = (row + 1) % 4, (row + 3) % 4, (row + 2) % 4
    rd, re = (row + 4 + dz) % 4, (row + 4 - dz) % 4
    yp, ym, yf = (y + 1) % 4, (y + 3) % 4, (y + 2) % 4
    lp, lm, lf = (lay + 1) % 4, (lay + 3) % 4, (lay + 2) % 4

    def a_part(c, h, s):
        return a[h].at[pl.ds(c * 16 + s * 8, 8)]

    def b_part(r, h, s):
        return b[h].at[pl.ds(r * 16 + s * 8, 8)]

    cols_in = pltpu.make_async_copy(cols_hbm, cols, small.at[0])
    list_in = pltpu.make_async_copy(list_hbm, pairs, small.at[1])
    own_in = []
    for h in range(3):
        rows = x_hbm.at[:, pl.ds(FIRST[h], ROWS[h])]
        own_in.append((
            pltpu.make_async_copy(rows, a[h].at[pl.ds(col * 16, 16)], loc.at[h, 0]),
            pltpu.make_async_copy(rows, b[h].at[pl.ds(row * 16, 16)], loc.at[h, 1])))
    cols_in.start()
    for pair in own_in:
        for m in pair:
            m.start()
    list_in.start()

    barrier = pltpu.get_barrier_semaphore()
    chips = [(row, ((col // 2 + k) % 8) * 2 + core, lay) for k in range(1, 8)]
    ends = [(r, col, lay) for r in (rp, rm, rf)]
    peers = chips + ends + [(row, sib, lay), (rd, pcol, lay), (row, col, lp), (row, col, lm)]
    for p in peers:
        pl.semaphore_signal(barrier, inc=1, device_id=p, device_id_type=MESH)

    for h in range(3):
        b[h][ZERO] = jnp.zeros((ROWS[h], EDGE), jnp.bfloat16)

    pl.semaphore_wait(barrier, len(peers))

    started = []

    def copy_to(src, dst, ssem, rsem, dev):
        return pltpu.make_async_remote_copy(
            src_ref=src, dst_ref=dst, send_sem=ssem, recv_sem=rsem,
            device_id=dev, device_id_type=MESH)

    def send(src, dst, ssem, rsem, dev):
        d = copy_to(src, dst, ssem, rsem, dev)
        d.start()
        started.append(d)

    to_sib = (row, sib, lay)
    to_p, to_d, to_pd, to_e = (row, pcol, lay), (rd, col, lay), (rd, pcol, lay), (re, col, lay)
    to_yp, to_ym = (row, col_of(zl, yp), lay), (row, col_of(zl, ym), lay)

    used = [0]

    def next_sem():
        used[0] += 1
        return gsend.at[used[0] - 1]

    def send_a(c, h, s, dev):
        send(a_part(c, h, s), a_part(c, h, s), next_sem(), a_recv.at[h, c, s], dev)

    def send_b(r, h, s, dev):
        send(b_part(r, h, s), b_part(r, h, s), next_sem(), b_recv.at[h, r, s], dev)

    def wait_a(c, h, s):
        copy_to(a_part(c, h, s), a_part(c, h, s), gsend.at[0], a_recv.at[h, c, s], to_sib).wait_recv()

    def wait_b(r, h, s):
        copy_to(b_part(r, h, s), b_part(r, h, s), gsend.at[0], b_recv.at[h, r, s], to_sib).wait_recv()

    def own_to(h, step):
        if step == "zp1":
            send_a(col, h, zl, to_p)
        elif step == "zp2":
            send_a(col, h, zp, to_p)
        elif step == "y0":
            send_a(col, h, 0, to_yp)
            send_a(col, h, 1, to_ym)
        elif step == "y1":
            send_a(col, h, 1, to_yp)
            send_a(col, h, 0, to_ym)
        elif step == "d1":
            send_b(row, h, zp, to_d)
        elif step == "d2":
            send_b(row, h, zl, to_d)
        elif step == "sb":
            send_a(col, h, 0, to_sib)
            send_a(col, h, 1, to_sib)
        elif step == "list":
            to_smem.wait()
        elif step == "in":
            for m in own_in[h]:
                m.wait()

    def pass_p(h, s):
        wait_a(pcol, h, s)
        send_a(pcol, h, s, to_yp)
        send_a(pcol, h, s, to_ym)
        send(a_part(pcol, h, s), b_part(row, h, s), next_sem(), b_recv.at[h, row, s], to_pd)
        send_a(pcol, h, s, to_sib)

    def pass_y(h, z):
        cm, cp = col_of(z, ym), col_of(z, yp)
        wait_a(cm, h, 0)
        send_a(cm, h, 0, to_yp)
        wait_a(cp, h, 1)
        send_a(cp, h, 1, to_ym)
        send_a(cm, h, 0, to_sib)
        send_a(cp, h, 1, to_sib)

    def rest_y(h, z):
        cm, cp = col_of(z, ym), col_of(z, yp)
        wait_a(cm, h, 1)
        send_a(cm, h, 1, to_sib)
        wait_a(cp, h, 0)
        send_a(cp, h, 0, to_sib)

    def far_y(h, z):
        cf = col_of(z, yf)
        for s in range(2):
            wait_a(cf, h, s)
            send_a(cf, h, s, to_sib)

    def far_b(h, which):
        if which == 0:
            wait_b(re, h, zp)
            send_b(re, h, zp, to_d)
        else:
            wait_b(rd, h, zl)
            send_b(rd, h, zl, to_e)

    def last_a(h):
        for z in range(2):
            for yy in range(4):
                c = (z * 4 + yy) * 2 + 1 - core
                wait_a(c, h, 0)
                wait_a(c, h, 1)

    def last_b(h):
        wait_b(re, h, zl)
        wait_b(rd, h, zp)
        wait_b(rf, h, 0)
        wait_b(rf, h, 1)

    lane = lax.broadcasted_iota(jnp.int32, (8, EDGE), 1)

    def columns():
        cols_in.wait()
        sub = lax.broadcasted_iota(jnp.int32, (8, EDGE), 0)
        for first, where in ((col * 4, ca.at[core, cidx]), (row * 4, cb.at[row])):
            vals = jnp.zeros((8, EDGE), jnp.int32)
            for s in range(2):
                for k in range(4):
                    for p in range(2):
                        vals = jnp.where((lane == first + k) & (sub == s * 2 + p), cols[s, p, k], vals)
            where[...] = vals
        for n, dev in enumerate(chips):
            send(ca.at[core, cidx], ca.at[core, cidx], csend.at[n], ca_recv.at[cidx], dev)
        for n, dev in enumerate(ends):
            send(cb.at[row], cb.at[row], csend.at[7 + n], cb_recv.at[row], dev)

    to_smem = pltpu.make_async_copy(idv, idx, small.at[2])

    def lists():
        for k in range(1, 8):
            ci = (cidx + k) % 8
            copy_to(ca.at[core, ci], ca.at[core, ci], csend.at[0], ca_recv.at[ci], to_sib).wait_recv()
        send(ca.at[core], ca.at[core], csend.at[10], ca_recv.at[8], to_sib)

    def places():
        for r in (rp, rm, rf):
            copy_to(cb.at[r], cb.at[r], csend.at[0], cb_recv.at[r], to_sib).wait_recv()
        copy_to(ca.at[1 - core], ca.at[1 - core], csend.at[0], ca_recv.at[8], to_sib).wait_recv()
        list_in.wait()
        acols = jnp.sum(ca[...].reshape(16, 8, EDGE), axis=0)
        bcols = jnp.sum(cb[...], axis=0)
        live = count[0, 0]
        for g in range(2):
            part = slice(g * EDGE, (g + 1) * EDGE)
            av = jnp.broadcast_to(pairs[0:1, part], (8, EDGE))
            bv = jnp.broadcast_to(pairs[1:2, part], (8, EDGE))
            have = jnp.take_along_axis(acols, av, axis=1, mode="promise_in_bounds")
            want = jnp.take_along_axis(bcols, bv, axis=1, mode="promise_in_bounds")
            ra, rb = av[0:1], bv[0:1]
            idv[0:1, part] = (ra >> 2) * 16 + (ra & 3) * 2
            alive = (lane[0:1] + g * EDGE) < live
            for s in range(2):
                base = (rb >> 2) * 16 + s * 8 + (rb & 3) * 2
                w0, w1 = want[s * 2 : s * 2 + 1], want[s * 2 + 1 : s * 2 + 2]
                for p in range(2):
                    q = s * 2 + p
                    h0 = have[q : q + 1]
                    at = jnp.where(h0 == w0, base, jnp.where(h0 == w1, base + 1, ZERO))
                    idv[1 + q : 2 + q, part] = jnp.where(alive, at, ZERO)
        idv[5:8, :] = jnp.zeros((3, 256), jnp.int32)
        to_smem.start()

    steps = {
        "p1": lambda h: pass_p(h, zp), "p2": lambda h: pass_p(h, zl),
        "q1": lambda h: pass_y(h, zl), "q2": lambda h: pass_y(h, zp),
        "r1": lambda h: rest_y(h, zl), "r2": lambda h: rest_y(h, zp),
        "f1": lambda h: far_y(h, zl), "f2": lambda h: far_y(h, zp),
        "b0": lambda h: far_b(h, 0), "b1": lambda h: far_b(h, 1), "lastA": last_a, "lastB": last_b,
        "cols": lambda h: columns(), "lists": lambda h: lists(), "places": lambda h: places(),
    }

    def left_of(t, h):
        u = idx[0, t]
        return jnp.concatenate([a[h][u], a[h][u + 1], a[h][u + 8], a[h][u + 9]], axis=1)

    def right_of(t, h):
        return jnp.concatenate([b[h][idx[1 + q, t]] for q in range(4)], axis=1)

    def times(left, right):
        return lax.dot_general(left, right, (((1,), (1,)), ((), ())),
                               preferred_element_type=jnp.float32)

    low = lax.broadcasted_iota(jnp.int32, (96, EDGE), 1) < HALF

    def quadrants(t):
        both = times(jnp.concatenate([left_of(t, 0), left_of(t + 1, 0)], axis=0),
                     jnp.concatenate([right_of(t, 0), right_of(t + 1, 0)], axis=0))
        return jnp.where(low[:HALF], both[:HALF], both[HALF:])

    def strips(t):
        both = times(jnp.concatenate([left_of(t, 1), left_of(t + 1, 1)], axis=0),
                     jnp.concatenate([right_of(t, 0), right_of(t + 1, 0)], axis=0))
        return jnp.where(low[:32], both[:32], both[32:])

    def whole(t):
        return times(jnp.concatenate([left_of(t, h) for h in range(3)], axis=0),
                     jnp.concatenate([right_of(t, h) for h in range(3)], axis=0))

    def rest(t):
        one, two = whole(t), whole(t + 1)
        mixed = jnp.where(low, pltpu.roll(two[:96], HALF, 1), one[:96])
        return jnp.concatenate([mixed, one[96:], two[96:]], axis=0)

    def half(v):
        return v.astype(jnp.bfloat16)

    def wide(v):
        return v.astype(jnp.float32)

    def each(n, body, unroll):
        def step(i, carry):
            for u in range(unroll):
                body(i * unroll + u)
            return carry
        lax.fori_loop(0, n // unroll, step, 0)

    def loop(n, body):
        def step(k, carry):
            body(k)
            return carry
        lax.fori_loop(0, n, step, 0)

    ring = [(row, col, lp), (row, col, lm)]
    next_owner = (lp, lm)

    class Piece:
        def __init__(self, refs, sems, value, unroll):
            self.f_out, self.f_in, self.n_out, self.n_in = refs
            self.f_send, self.f_recv, self.n_send, self.n_recv = sems
            self.value, self.unroll = value, unroll
            self.parts = self.f_send.shape[1]
            self.chunk = PAIRS // self.parts

        def f_copy(self, d, k):
            part = pl.ds(k * self.chunk, self.chunk)
            return copy_to(self.f_out.at[d, part], self.f_in.at[d, part],
                           self.f_send.at[d, k], self.f_recv.at[d, k], ring[d])

        def n_copy(self, d, g, k):
            part = pl.ds(k * self.chunk, self.chunk)
            return copy_to(self.n_out.at[d, g, part], self.n_in.at[d, g, part],
                           self.n_send.at[d, g, k], self.n_recv.at[d, g, k], ring[d])

        def far(self, k):
            for d in range(2):
                def body(i):
                    j = k * self.chunk + i
                    self.f_out[d, j] = half(self.value(lf * 64 + d * 32 + 2 * j))
                each(self.chunk, body, self.unroll)
                self.f_copy(d, k).start()

        def near(self, k):
            for d in range(2):
                g = 1 - d
                def body(i):
                    j = k * self.chunk + i
                    self.n_out[d, g, j] = half(self.value(next_owner[d] * 64 + g * 32 + 2 * j))
                each(self.chunk, body, self.unroll)
                self.n_copy(d, g, k).start()

        def sum(self, k):
            for d in range(2):
                self.f_copy(d, k).wait_recv()
                def body(i):
                    j = k * self.chunk + i
                    own = self.value(next_owner[d] * 64 + d * 32 + 2 * j)
                    self.n_out[d, d, j] = half(own + wide(self.f_in[d, j]))
                each(self.chunk, body, self.unroll)
                self.n_copy(d, d, k).start()

        def arrived(self, g, k):
            for d in range(2):
                self.n_copy(d, g, k).wait_recv()

        def sent(self):
            for d in range(2):
                loop(self.parts, lambda k: self.f_copy(d, k).wait_send())
                for g in range(2):
                    loop(self.parts, lambda k: self.n_copy(d, g, k).wait_send())

        def total(self, g, j):
            return wide(self.n_in[0, g, j]) + wide(self.n_in[1, g, j])

    corner = Piece(q_refs, q_sems, quadrants, 4)
    strip = Piece(s_refs, s_sems, strips, 4)
    remainder = Piece(r_refs, r_sems, rest, 2)

    def mine(t):
        out_ref[t] = whole(lay * 64 + t)

    def remaining():
        loop(remainder.parts, remainder.far)
        loop(remainder.parts, remainder.near)
        each(64, mine, 4)
        loop(remainder.parts, remainder.sum)

    kinds = {"F": corner.far, "N": corner.near, "S": corner.sum,
             "f": strip.far, "n": strip.near, "s": strip.sum}
    for word in ORDER:
        if word == "R":
            remaining()
        elif word[0] in kinds:
            kinds[word[0]](int(word[1:] or 0))
        elif word[1:] in steps:
            steps[word[1:]](int(word[0]))
        else:
            own_to(int(word[0]), word[1:])

    for g in range(2):
        for piece in (corner, strip):
            loop(piece.parts, lambda k: piece.arrived(g, k))

    def finish(k):
        for g in range(2):
            remainder.arrived(g, k)

            def body(i):
                j = k * remainder.chunk + i
                t = g * 32 + 2 * j
                first = jnp.concatenate([corner.total(g, j), strip.total(g, j)], axis=0)
                more = remainder.total(g, j)
                mixed = more[:96]
                upper, lower = pl.ds(0, 96), pl.ds(96, 32)
                out_ref[t, upper] += jnp.where(low, first, mixed)
                out_ref[t, lower] += more[96:128]
                out_ref[t + 1, upper] += pltpu.roll(jnp.where(low, mixed, first), HALF, 1)
                out_ref[t + 1, lower] += more[128:]

            each(remainder.chunk, body, 2)

    loop(remainder.parts, finish)

    for d in started:
        d.wait_send()
    for piece in (corner, strip, remainder):
        piece.sent()


def on_device(x_tiles, x_cols, c_list, c_count):
    hbm = pl.BlockSpec(memory_space=pltpu.HBM)
    dma = pltpu.SemaphoreType.DMA
    bf16 = lambda *dims: pltpu.VMEM(dims + (EDGE,), jnp.bfloat16)
    ints = lambda *dims: pltpu.VMEM(dims, jnp.int32)
    buffers = lambda n: [bf16(2, PAIRS, n), bf16(2, PAIRS, n), bf16(2, 2, PAIRS, n), bf16(2, 2, PAIRS, n)]
    semaphores = lambda n: [dma((2, n)), dma((2, n)), dma((2, 2, n)), dma((2, 2, n))]
    operands = [
        pltpu.with_memory_space_constraint(v, pltpu.HBM)
        for v in (x_tiles.reshape(16, EDGE, EDGE), jnp.swapaxes(x_cols, 1, 2),
                  jnp.swapaxes(c_list[0, 0], 0, 1))
    ]
    out = pl.pallas_call(
        kernel,
        out_shape=pltpu.VMEM((64, EDGE, EDGE), jnp.float32),
        in_specs=[hbm] * 3 + [pl.BlockSpec(memory_space=pltpu.SMEM)],
        out_specs=pl.BlockSpec(memory_space=pltpu.VMEM),
        scratch_shapes=[
            *[bf16(A_UNITS, n) for n in ROWS], *[bf16(B_UNITS, n) for n in ROWS],
            buffers(64), buffers(32), buffers(160),
            ints(2, 8, 8, EDGE), ints(4, 8, EDGE),
            pltpu.SMEM((2, 2, 4), jnp.int32), ints(2, 256),
            ints(8, 256), pltpu.SMEM((8, 256), jnp.int32),
            dma((3, 2)), dma((3,)), dma((108,)), dma((3, 16, 2)), dma((3, 4, 2)),
            dma((11,)), dma((9,)), dma((4,)),
            semaphores(Q_PARTS), semaphores(S_PARTS), semaphores(R_PARTS),
        ],
        compiler_params=pltpu.CompilerParams(
            collective_id=0, has_side_effects=True, vmem_limit_bytes=40 * 1024 * 1024),
    )(*operands, c_count)
    return out[None, None]


def solution(mesh):
    return jax.shard_map(
        on_device,
        mesh=mesh,
        in_specs=(
            P("layer", ("row", "col"), None, None, None),
            P("layer", ("row", "col"), None),
            P("row", "col", None, None),
            P("row", "col"),
        ),
        out_specs=P("row", "col", "layer", None, None),
        check_vma=False,
    )
```

time: 115 us -> 111 us (0.965)
  Pallas kernels: 113 us -> 109 us
    pallas_call x1, Pallas kernels: 113 us -> 109 us  [on_device(): pl.pallas_call(kernel, out_shape=pltpu.VMEM((64, EDGE, EDGE), jnp.float32...]
where the time goes in v3:
time: 111 us
  Pallas kernels  109 us (98%)
  local copies, waits for them, and re-layouts  2.02 us (2%)
    pallas_call x1, Pallas kernels, on_device(): pl.pallas_call(kernel, out_shape=pltpu.VMEM((64, EDGE, EDGE), jnp.float32...  109 us

profile of v3, /device:TPU:1, one launch (start us, length us, event | category | flops | bytes accessed | tf_op | source)
XLA Modules:
  0.0 111.3 jit_solution(12183711642418015872)
XLA Ops:
  0.7 108.6 %shard_map.46 = f32[64,128,128]{2,1,0:T(8,128)S(1)} custom-call(bf16[16,128,128]{2,1,0:T(8,128)(2,1)} %bitcast.7, s32[2,2,4]{2,1,0:T(2,128)} %bitcast.8, s32[2,256]{1,0:T(2,128)} %bitcast.9, s32[1,1]{1,0:T(1,128)S(6)} %copy.7.count), custom_call_target="tpu_custom_call" | custom-call | tf_op jit(solution)/shard_map/pallas_call | solution.py:433
  109.3 2.0 %copy.6 = f32[1,1,64,128,128]{4,3,2,1,0:T(8,128)} copy(f32[1,1,64,128,128]{4,3,2,1,0:T(8,128)S(1)} %bitcast.6) | data formatting | bytes 8388608

commit v4 on v3

--- a/solution.py
+++ b/solution.py
@@ -13,16 +13,15 @@
 B_UNITS = 65
 ZERO = 64
 PAIRS = 16
-Q_PARTS, S_PARTS, R_PARTS = 4, 2, 4
+Q_PARTS, S_PARTS, R_PARTS = 2, 1, 4
 MESH = pl.DeviceIdType.MESH
 ORDER = (
     "0in", "0zp1", "0zp2", "0y0", "0y1", "0sb", "0d1", "0cols", "0q1", "0p1", "0d2", "0lists",
-    "0p2", "0r1", "0b1", "0places", "0q2", "1in", "1y0", "1y1", "1zp1", "1zp2", "0b0", "1d1",
-    "1d2", "1sb", "0r2", "0f1", "0f2", "0lastA", "0lastB", "0list", "F0", "F1", "1q1", "1p1",
-    "F2", "F3", "1p2", "N0", "N1", "1r1", "2in", "2y0", "2y1", "2zp1", "2zp2", "2sb", "1b1",
-    "1b0", "1q2", "N2", "N3", "2d1", "2d2", "S0", "S1", "2q1", "2p1", "S2", "S3", "1r2", "1f1",
-    "1f2", "1lastA", "2p2", "f0", "f1", "2r1", "n0", "n1", "2b1", "2b0", "2q2", "s0", "s1",
-    "2r2", "2f1", "2f2", "2lastA", "1lastB", "2lastB", "R",
+    "0p2", "0r1", "0b1", "0places", "0q2", "1in", "1y0", "1y1", "0b0", "1zp1", "1zp2", "0r2",
+    "0f1", "0f2", "0lastA", "0lastB", "0list", "F0", "1sb", "1d1", "1d2", "F1", "1q1", "N0",
+    "1p1", "N1", "1p2", "1r1", "2in", "2y0", "2y1", "2zp1", "2zp2", "2sb", "1b1", "S0", "1b0",
+    "1q2", "S1", "2d1", "2d2", "2q1", "2p1", "1r2", "1f1", "1f2", "1lastA", "f0", "2p2", "2r1",
+    "n0", "2b1", "2b0", "2q2", "s0", "2r2", "2f1", "2f2", "2lastA", "1lastB", "2lastB", "R",
 )
 
 
@@ -302,8 +301,11 @@
             return carry
         lax.fori_loop(0, n, step, 0)
 
-    ring = [(row, col, lp), (row, col, lm)]
-    next_owner = (lp, lm)
+    def next_owner(d):
+        return (lay + 1 + 2 * d) % 4
+
+    def towards(d):
+        return (row, col, next_owner(d))
 
     class Piece:
         def __init__(self, refs, sems, value, unroll):
@@ -316,56 +318,60 @@
         def f_copy(self, d, k):
             part = pl.ds(k * self.chunk, self.chunk)
             return copy_to(self.f_out.at[d, part], self.f_in.at[d, part],
-                           self.f_send.at[d, k], self.f_recv.at[d, k], ring[d])
+                           self.f_send.at[d, k], self.f_recv.at[d, k], towards(d))
 
         def n_copy(self, d, g, k):
             part = pl.ds(k * self.chunk, self.chunk)
             return copy_to(self.n_out.at[d, g, part], self.n_in.at[d, g, part],
-                           self.n_send.at[d, g, k], self.n_recv.at[d, g, k], ring[d])
+                           self.n_send.at[d, g, k], self.n_recv.at[d, g, k], towards(d))
 
         def far(self, k):
-            for d in range(2):
+            def way(d):
                 def body(i):
                     j = k * self.chunk + i
                     self.f_out[d, j] = half(self.value(lf * 64 + d * 32 + 2 * j))
                 each(self.chunk, body, self.unroll)
                 self.f_copy(d, k).start()
+            loop(2, way)
 
         def near(self, k):
-            for d in range(2):
+            def way(d):
                 g = 1 - d
                 def body(i):
                     j = k * self.chunk + i
-                    self.n_out[d, g, j] = half(self.value(next_owner[d] * 64 + g * 32 + 2 * j))
+                    self.n_out[d, g, j] = half(self.value(next_owner(d) * 64 + g * 32 + 2 * j))
                 each(self.chunk, body, self.unroll)
                 self.n_copy(d, g, k).start()
+            loop(2, way)
 
         def sum(self, k):
-            for d in range(2):
+            def way(d):
                 self.f_copy(d, k).wait_recv()
                 def body(i):
                     j = k * self.chunk + i
-                    own = self.value(next_owner[d] * 64 + d * 32 + 2 * j)
+                    own = self.value(next_owner(d) * 64 + d * 32 + 2 * j)
                     self.n_out[d, d, j] = half(own + wide(self.f_in[d, j]))
                 each(self.chunk, body, self.unroll)
                 self.n_copy(d, d, k).start()
+            loop(2, way)
 
         def arrived(self, g, k):
             for d in range(2):
                 self.n_copy(d, g, k).wait_recv()
 
-        def sent(self):
-            for d in range(2):
-                loop(self.parts, lambda k: self.f_copy(d, k).wait_send())
-                for g in range(2):
-                    loop(self.parts, lambda k: self.n_copy(d, g, k).wait_send())
+        def far_sent(self):
+            loop(2, lambda d: loop(self.parts, lambda k: self.f_copy(d, k).wait_send()))
+
+        def near_sent(self):
+            loop(2, lambda d: loop(
+                2, lambda g: loop(self.parts, lambda k: self.n_copy(d, g, k).wait_send())))
 
         def total(self, g, j):
             return wide(self.n_in[0, g, j]) + wide(self.n_in[1, g, j])
 
-    corner = Piece(q_refs, q_sems, quadrants, 4)
-    strip = Piece(s_refs, s_sems, strips, 4)
-    remainder = Piece(r_refs, r_sems, rest, 2)
+    corner = Piece(q_refs, q_sems, quadrants, 8)
+    strip = Piece(s_refs, s_sems, strips, 8)
+    remainder = Piece(r_refs, r_sems, rest, 4)
 
     def mine(t):
         out_ref[t] = whole(lay * 64 + t)
@@ -373,7 +379,7 @@
     def remaining():
         loop(remainder.parts, remainder.far)
         loop(remainder.parts, remainder.near)
-        each(64, mine, 4)
+        each(64, mine, 8)
         loop(remainder.parts, remainder.sum)
 
     kinds = {"F": corner.far, "N": corner.near, "S": corner.sum,
@@ -388,12 +394,19 @@
         else:
             own_to(int(word[0]), word[1:])
 
+    for d in started:
+        d.wait_send()
+    for piece in (corner, strip):
+        piece.far_sent()
+        piece.near_sent()
+    remainder.far_sent()
+
     for g in range(2):
         for piece in (corner, strip):
             loop(piece.parts, lambda k: piece.arrived(g, k))
 
     def finish(k):
-        for g in range(2):
+        def group(g):
             remainder.arrived(g, k)
 
             def body(i):
@@ -408,14 +421,13 @@
                 out_ref[t + 1, upper] += pltpu.roll(jnp.where(low, mixed, first), HALF, 1)
                 out_ref[t + 1, lower] += more[128:]
 
-            each(remainder.chunk, body, 2)
+            each(remainder.chunk, body, 4)
+
+        loop(2, group)
 
     loop(remainder.parts, finish)
 
-    for d in started:
-        d.wait_send()
-    for piece in (corner, strip, remainder):
-        piece.sent()
+    remainder.near_sent()
 
 
 def on_device(x_tiles, x_cols, c_list, c_count):

time: 111 us -> 110 us (level)
  Pallas kernels: 109 us -> 107 us
    pallas_call x1, Pallas kernels: 109 us -> 107 us  [on_device(): pl.pallas_call(kernel, out_shape=pltpu.VMEM((64, EDGE, EDGE), jnp.float32...]
where the time goes in v4:
time: 110 us
  Pallas kernels  107 us (97%)
  local copies, waits for them, and re-layouts  2.02 us (2%)
    pallas_call x1, Pallas kernels, on_device(): pl.pallas_call(kernel, out_shape=pltpu.VMEM((64, EDGE, EDGE), jnp.float32...  107 us

profile of v4, /device:TPU:1, one launch (start us, length us, event | category | flops | bytes accessed | tf_op | source)
XLA Modules:
  0.0 110.0 jit_solution(665826806912851588)
XLA Ops:
  0.7 107.4 %shard_map.46 = f32[64,128,128]{2,1,0:T(8,128)S(1)} custom-call(bf16[16,128,128]{2,1,0:T(8,128)(2,1)} %bitcast.7, s32[2,2,4]{2,1,0:T(2,128)} %bitcast.8, s32[2,256]{1,0:T(2,128)} %bitcast.9, s32[1,1]{1,0:T(1,128)S(6)} %copy.7.count), custom_call_target="tpu_custom_call" | custom-call | tf_op jit(solution)/shard_map/pallas_call | solution.py:445
  108.0 2.0 %copy.6 = f32[1,1,64,128,128]{4,3,2,1,0:T(8,128)} copy(f32[1,1,64,128,128]{4,3,2,1,0:T(8,128)S(1)} %bitcast.6) | data formatting | bytes 8388608

commit v5 on v4

--- a/solution.py
+++ b/solution.py
@@ -17,8 +17,8 @@
 MESH = pl.DeviceIdType.MESH
 ORDER = (
     "0in", "0zp1", "0zp2", "0y0", "0y1", "0sb", "0d1", "0cols", "0q1", "0p1", "0d2", "0lists",
-    "0p2", "0r1", "0b1", "0places", "0q2", "1in", "1y0", "1y1", "0b0", "1zp1", "1zp2", "0r2",
-    "0f1", "0f2", "0lastA", "0lastB", "0list", "F0", "1sb", "1d1", "1d2", "F1", "1q1", "N0",
+    "0p2", "0r1", "0b1", "0b0", "0f1", "0places", "0q2", "1in", "1y0", "1y1", "1zp1", "1zp2",
+    "0r2", "0f2", "0lastA", "0lastB", "0list", "F0", "1sb", "1d1", "1d2", "F1", "1q1", "N0",
     "1p1", "N1", "1p2", "1r1", "2in", "2y0", "2y1", "2zp1", "2zp2", "2sb", "1b1", "S0", "1b0",
     "1q2", "S1", "2d1", "2d2", "2q1", "2p1", "1r2", "1f1", "1f2", "1lastA", "f0", "2p2", "2r1",
     "n0", "2b1", "2b0", "2q2", "s0", "2r2", "2f1", "2f2", "2lastA", "1lastB", "2lastB", "R",

time: 110 us -> 110 us (level)
  no operation moved by 1% of the time
where the time goes in v5:
time: 110 us
  Pallas kernels  107 us (97%)
  local copies, waits for them, and re-layouts  2.02 us (2%)
    pallas_call x1, Pallas kernels, on_device(): pl.pallas_call(kernel, out_shape=pltpu.VMEM((64, EDGE, EDGE), jnp.float32...  107 us

profile of v5, /device:TPU:1, one launch (start us, length us, event | category | flops | bytes accessed | tf_op | source)
XLA Modules:
  0.0 109.6 jit_solution(7894085785601907807)
XLA Ops:
  0.7 106.9 %shard_map.46 = f32[64,128,128]{2,1,0:T(8,128)S(1)} custom-call(bf16[16,128,128]{2,1,0:T(8,128)(2,1)} %bitcast.7, s32[2,2,4]{2,1,0:T(2,128)} %bitcast.8, s32[2,256]{1,0:T(2,128)} %bitcast.9, s32[1,1]{1,0:T(1,128)S(6)} %copy.7.count), custom_call_target="tpu_custom_call" | custom-call | tf_op jit(solution)/shard_map/pallas_call | solution.py:445
  107.5 2.0 %copy.6 = f32[1,1,64,128,128]{4,3,2,1,0:T(8,128)} copy(f32[1,1,64,128,128]{4,3,2,1,0:T(8,128)S(1)} %bitcast.6) | data formatting | bytes 8388608

commit v6 on v5

--- a/solution.py
+++ b/solution.py
@@ -19,9 +19,9 @@
     "0in", "0zp1", "0zp2", "0y0", "0y1", "0sb", "0d1", "0cols", "0q1", "0p1", "0d2", "0lists",
     "0p2", "0r1", "0b1", "0b0", "0f1", "0places", "0q2", "1in", "1y0", "1y1", "1zp1", "1zp2",
     "0r2", "0f2", "0lastA", "0lastB", "0list", "F0", "1sb", "1d1", "1d2", "F1", "1q1", "N0",
-    "1p1", "N1", "1p2", "1r1", "2in", "2y0", "2y1", "2zp1", "2zp2", "2sb", "1b1", "S0", "1b0",
+    "1p1", "N1", "1p2", "1r1", "2in", "2y0", "2y1", "2zp1", "2zp2", "2sb", "1b0", "S0", "1b1",
     "1q2", "S1", "2d1", "2d2", "2q1", "2p1", "1r2", "1f1", "1f2", "1lastA", "f0", "2p2", "2r1",
-    "n0", "2b1", "2b0", "2q2", "s0", "2r2", "2f1", "2f2", "2lastA", "1lastB", "2lastB", "R",
+    "n0", "2b0", "2b1", "2q2", "s0", "2r2", "2f1", "2f2", "2lastA", "1lastB", "2lastB", "R",
 )
 
 

time: 110 us -> 110 us (level)
  no operation moved by 1% of the time
where the time goes in v6:
time: 110 us
  Pallas kernels  107 us (97%)
  local copies, waits for them, and re-layouts  2.02 us (2%)
    pallas_call x1, Pallas kernels, on_device(): pl.pallas_call(kernel, out_shape=pltpu.VMEM((64, EDGE, EDGE), jnp.float32...  107 us

profile of v6, /device:TPU:1, one launch (start us, length us, event | category | flops | bytes accessed | tf_op | source)
XLA Modules:
  0.0 109.6 jit_solution(9967380363022697011)
XLA Ops:
  0.7 106.9 %shard_map.46 = f32[64,128,128]{2,1,0:T(8,128)S(1)} custom-call(bf16[16,128,128]{2,1,0:T(8,128)(2,1)} %bitcast.7, s32[2,2,4]{2,1,0:T(2,128)} %bitcast.8, s32[2,256]{1,0:T(2,128)} %bitcast.9, s32[1,1]{1,0:T(1,128)S(6)} %copy.7.count), custom_call_target="tpu_custom_call" | custom-call | tf_op jit(solution)/shard_map/pallas_call | solution.py:445
  107.5 2.0 %copy.6 = f32[1,1,64,128,128]{4,3,2,1,0:T(8,128)} copy(f32[1,1,64,128,128]{4,3,2,1,0:T(8,128)S(1)} %bitcast.6) | data formatting | bytes 8388608
